TPU v7x, 512 devices: a whole 4x4x16 slice. The times are simulated.
512 devices in a mesh: segment: 8 (over y, core), rows: 16 (over z), dp: 4 (over x).
Axes of the slice: x: 4, y: 4, z: 16, core: 2. Of those that a mesh axis runs over, the one named last changes fastest.
Arguments:
- clips: bfloat16 [4, 4, 4, 128, 8, 128], P(None, 'dp', None, 'rows'), may hold values from -80 to 80
- lengths: int32 [4, 4], P(None, 'dp'), may hold values from 1 to 4, as said below
- conv_weight: bfloat16 [8, 3456, 128], P('segment'), may hold values from -0.109375 to 0.109375
- norm_gain: float32 [8, 128], P('segment'), may hold values from 0.5 to 2
- norm_shift: float32 [8, 128], P('segment'), may hold values from -1 to 1
- conv_bias: float32 [8, 128], P('segment'), may hold values from -3 to 3
- cotangent: bfloat16 [8, 4, 4, 4, 128, 8, 128], P('segment', None, 'dp', None, 'rows'), may hold values from -6 to 6
Outputs:
- stash: bfloat16 [8, 4, 4, 4, 128, 8, 128], P('segment', None, 'dp', None, 'rows')
- weight_grad: float32 [8, 3456, 128], P('segment')
Inputs may be any that keep to these rules, and one draw needn't show every extreme that they name: lengths[m, clip] real frames lead each clip; the frames after them are padding; some clip has all 4 frames.
All inputs are finite; a program needn't handle non-finite values.
Results may differ from a plain program's by a relative error of at most 0.009.
Values may be sent and summed in bfloat16 or wider, within the bound.
A program may use at most 64 MiB of HBM per device.

v0:
```python
import math
import jax
import jax.numpy as jnp
from jax import lax
from jax.sharding import PartitionSpec as P

GROUPS = 32
eps = 1e-06


def extended_2(cells, sides, width):
    for axis, dim in sides:
        count = lax.axis_size(axis)
        ends = count - 1
        head = lax.slice_in_dim(cells, 0, width, axis=dim)
        tail = lax.slice_in_dim(cells, cells.shape[dim] - width, cells.shape[dim], axis=dim)
        cells = jnp.concatenate(
            [
                lax.ppermute(tail, axis, [(i, (i + 1) % count) for i in range(ends)]),
                cells,
                lax.ppermute(head, axis, [((i + 1) % count, i) for i in range(ends)]),
            ],
            axis=dim,
        )
    return cells


def passed_along(block, axis, distance):
    devices = range(lax.axis_size(axis))
    route = [(i - distance, i) for i in devices if i - distance in devices]
    return lax.ppermute(block, axis, route)


def statistics(values, frame_mask, length, height):
    clip_count, frames, rows_here, cols, chans = values.shape
    sub = chans // GROUPS
    grouped = values.reshape(clip_count, frames, rows_here, cols, GROUPS, sub)
    mask_six = frame_mask[:, :, :, :, :, None]
    count = (length * (height * cols * sub)).astype(jnp.float32)[:, None]
    total = lax.psum(jnp.sum(grouped * mask_six, axis=(1, 2, 3, 5)), "rows")
    mean = total / count
    centered = grouped - mean[:, None, None, None, :, None]
    spread = lax.psum(jnp.sum(centered * centered * mask_six, axis=(1, 2, 3, 5)), "rows")
    var = spread / count
    rstd = lax.rsqrt(var + eps)
    mean_chan = jnp.repeat(mean, sub, axis=-1)[:, None, None, None, :]
    rstd_chan = jnp.repeat(rstd, sub, axis=-1)[:, None, None, None, :]
    return (mean_chan, rstd_chan)


def block(current, length, weight, gain, shift, bias, height):
    clip_count, frames, rows_here, cols, chans = current.shape
    values = current.astype(jnp.float32)
    frame_mask = (jnp.arange(frames)[None, :] < length[:, None]).astype(jnp.float32)[
        :, :, None, None, None
    ]
    mean_chan, rstd_chan = statistics(values, frame_mask, length, height)
    hidden = jax.nn.silu((values - mean_chan) * rstd_chan * gain + shift).astype(jnp.bfloat16)
    extended = extended_2(hidden, (("rows", 2),), 1)
    padded = jnp.pad(extended, ((0, 0), (0, 0), (0, 0), (1, 1), (0, 0)))
    padded = jnp.concatenate([padded[:, :1], padded[:, :1], padded], axis=1)
    pieces = []
    for tap_t in range(3):
        for tap_h in range(3):
            for tap_w in range(3):
                pieces.append(
                    padded[
                        :,
                        tap_t : tap_t + frames,
                        tap_h : tap_h + rows_here,
                        tap_w : tap_w + cols,
                        :,
                    ]
                )
    patches = jnp.concatenate(pieces, axis=-1).reshape(-1, 27 * chans)
    conv = jnp.dot(patches, weight, preferred_element_type=jnp.float32).reshape(values.shape)
    result = ((values + conv + bias) * frame_mask).astype(jnp.bfloat16)
    return (result, patches, frame_mask.astype(jnp.bfloat16))


def per_device(clips, lengths, conv_weight, norm_gain, norm_shift, conv_bias, cotangent):
    segments = lax.axis_size("segment")
    segment_id = lax.axis_index("segment")
    micro = clips.shape[0]
    frames = clips.shape[2]
    cols = clips.shape[4]
    chans = clips.shape[5]
    height = clips.shape[3] * lax.axis_size("rows")
    weight = conv_weight[0]
    gain = norm_gain[0]
    shift = norm_shift[0]
    bias = conv_bias[0]
    cot_all = cotangent[0]
    total_cells = micro * clips.shape[1] * lax.axis_size("dp") * frames * height * cols
    factor = 1.0 / math.sqrt(total_cells)

    def tick(step, carry):
        arrived, stash, grads = carry
        which = step - segment_id
        valid = (which >= 0) & (which < micro)
        slot = jnp.clip(which, 0, micro - 1)
        fresh = lax.dynamic_index_in_dim(
            clips, jnp.clip(step, 0, micro - 1).astype(jnp.int32), 0, keepdims=False
        )
        current = jnp.where(segment_id == 0, fresh, arrived)
        length = lax.dynamic_index_in_dim(lengths, slot, 0, keepdims=False)
        result, patches, mask_five = block(current, length, weight, gain, shift, bias, height)
        cot_now = lax.dynamic_index_in_dim(cot_all, slot, 0, keepdims=False)
        masked = (cot_now * mask_five).reshape(-1, chans)
        term = lax.dot_general(
            patches, masked, (((0,), (0,)), ((), ())), preferred_element_type=jnp.float32
        )
        grads = grads + jnp.where(valid, term, 0.0)
        previous = lax.dynamic_index_in_dim(stash, slot, 0, keepdims=False)
        stash = lax.dynamic_update_index_in_dim(stash, jnp.where(valid, result, previous), slot, 0)
        arrived = passed_along(result, "segment", 1)
        return (arrived, stash, grads)

    start = (
        jnp.zeros(clips.shape[1:], jnp.bfloat16),
        jnp.zeros(clips.shape, jnp.bfloat16),
        jnp.zeros((27 * chans, chans), jnp.float32),
    )
    arrived, stash, grads = lax.fori_loop(0, micro + segments - 1, tick, start)
    grads = lax.psum(grads, ("rows", "dp")) * factor
    return (stash[None], grads[None])


def solution(mesh):
    in_specs = (
        P(None, "dp", None, "rows", None, None),
        P(None, "dp"),
        P("segment", None, None),
        P("segment", None),
        P("segment", None),
        P("segment", None),
        P("segment", None, "dp", None, "rows", None, None),
    )
    out_specs = (P("segment", None, "dp", None, "rows", None, None), P("segment", None, None))
    return jax.shard_map(
        per_device, mesh=mesh, in_specs=in_specs, out_specs=out_specs, check_vma=False
    )
```

profile of v0, /device:TPU:8, one launch (start us, length us, event | category | flops | bytes accessed | tf_op | source)
XLA Modules:
  0.0 1160.9 jit_solution(13718055022507466365)
XLA Ops:
  7.3 867.2 %while.20 = (s32[]{:T(128)}, bf16[1,4,8,8,128]{4,3,2,1,0:T(8,128)(2,1)S(1)}, bf16[4,1,4,8,8,128]{5,4,3,2,1,0:T(8,128)(2,1)S(1)}, f32[3456,128]{1,0:T(8,128)S(1)}...) while((s32[]{:T(128)}, ...), condition=%wide.region_7.8_spmd.clone, body=%wide.region_0.7_spmd.clone.sunk | while | flops 457701504 | bytes 18060908 | solution.py:124
  10.4 36.5 %psum.40 = f32[1,32]{1,0:T(1,128)S(1)} all-reduce(f32[1,32]{1,0:T(1,128)S(1)} %bitcast.110), channel_id=1, replica_groups=mesh['segment'=8,'rows'=16,'dp'=4] {'rows'}, use_global_device_ids=true, to_apply=%region_3.3 | all-reduce | flops 32 | bytes 256 | tf_op jit(solution)/shard_map/while/body/eval_jaxpr/psum | solution.py:40
  48.0 27.0 %psum.41 = f32[1,32]{1,0:T(1,128)S(1)} all-reduce(f32[1,32]{1,0:T(1,128)S(1)} %bitcast.109), channel_id=1, replica_groups=mesh['segment'=8,'rows'=16,'dp'=4] {'rows'}, use_global_device_ids=true, to_apply=%region_6.6 | all-reduce | flops 32 | bytes 256 | tf_op jit(solution)/shard_map/while/body/eval_jaxpr/psum | solution.py:43
  77.3 4.5 collective-permute-start.1
  87.5 2.3 fusion.108
  94.2 30.5 %psum.40 = f32[1,32]{1,0:T(1,128)S(1)} all-reduce(f32[1,32]{1,0:T(1,128)S(1)} %bitcast.110), channel_id=1, replica_groups=mesh['segment'=8,'rows'=16,'dp'=4] {'rows'}, use_global_device_ids=true, to_apply=%region_3.3 | all-reduce | flops 32 | bytes 256 | tf_op jit(solution)/shard_map/while/body/eval_jaxpr/psum | solution.py:40
  125.8 29.1 %psum.41 = f32[1,32]{1,0:T(1,128)S(1)} all-reduce(f32[1,32]{1,0:T(1,128)S(1)} %bitcast.109), channel_id=1, replica_groups=mesh['segment'=8,'rows'=16,'dp'=4] {'rows'}, use_global_device_ids=true, to_apply=%region_6.6 | all-reduce | flops 32 | bytes 256 | tf_op jit(solution)/shard_map/while/body/eval_jaxpr/psum | solution.py:43
  157.2 4.5 collective-permute-start.1
  167.3 2.3 fusion.108
  174.0 29.3 %psum.40 = f32[1,32]{1,0:T(1,128)S(1)} all-reduce(f32[1,32]{1,0:T(1,128)S(1)} %bitcast.110), channel_id=1, replica_groups=mesh['segment'=8,'rows'=16,'dp'=4] {'rows'}, use_global_device_ids=true, to_apply=%region_3.3 | all-reduce | flops 32 | bytes 256 | tf_op jit(solution)/shard_map/while/body/eval_jaxpr/psum | solution.py:40
  204.5 28.3 %psum.41 = f32[1,32]{1,0:T(1,128)S(1)} all-reduce(f32[1,32]{1,0:T(1,128)S(1)} %bitcast.109), channel_id=1, replica_groups=mesh['segment'=8,'rows'=16,'dp'=4] {'rows'}, use_global_device_ids=true, to_apply=%region_6.6 | all-reduce | flops 32 | bytes 256 | tf_op jit(solution)/shard_map/while/body/eval_jaxpr/psum | solution.py:43
  235.0 4.5 collective-permute-start.1
  245.2 2.3 fusion.108
  251.8 29.3 %psum.40 = f32[1,32]{1,0:T(1,128)S(1)} all-reduce(f32[1,32]{1,0:T(1,128)S(1)} %bitcast.110), channel_id=1, replica_groups=mesh['segment'=8,'rows'=16,'dp'=4] {'rows'}, use_global_device_ids=true, to_apply=%region_3.3 | all-reduce | flops 32 | bytes 256 | tf_op jit(solution)/shard_map/while/body/eval_jaxpr/psum | solution.py:40
  282.3 29.0 %psum.41 = f32[1,32]{1,0:T(1,128)S(1)} all-reduce(f32[1,32]{1,0:T(1,128)S(1)} %bitcast.109), channel_id=1, replica_groups=mesh['segment'=8,'rows'=16,'dp'=4] {'rows'}, use_global_device_ids=true, to_apply=%region_6.6 | all-reduce | flops 32 | bytes 256 | tf_op jit(solution)/shard_map/while/body/eval_jaxpr/psum | solution.py:43
  313.6 4.5 collective-permute-start.1
  323.8 2.3 fusion.108
  330.4 29.3 %psum.40 = f32[1,32]{1,0:T(1,128)S(1)} all-reduce(f32[1,32]{1,0:T(1,128)S(1)} %bitcast.110), channel_id=1, replica_groups=mesh['segment'=8,'rows'=16,'dp'=4] {'rows'}, use_global_device_ids=true, to_apply=%region_3.3 | all-reduce | flops 32 | bytes 256 | tf_op jit(solution)/shard_map/while/body/eval_jaxpr/psum | solution.py:40
  360.9 28.2 %psum.41 = f32[1,32]{1,0:T(1,128)S(1)} all-reduce(f32[1,32]{1,0:T(1,128)S(1)} %bitcast.109), channel_id=1, replica_groups=mesh['segment'=8,'rows'=16,'dp'=4] {'rows'}, use_global_device_ids=true, to_apply=%region_6.6 | all-reduce | flops 32 | bytes 256 | tf_op jit(solution)/shard_map/while/body/eval_jaxpr/psum | solution.py:43
  391.4 4.5 collective-permute-start.1
  401.6 2.3 fusion.108
  408.3 29.3 %psum.40 = f32[1,32]{1,0:T(1,128)S(1)} all-reduce(f32[1,32]{1,0:T(1,128)S(1)} %bitcast.110), channel_id=1, replica_groups=mesh['segment'=8,'rows'=16,'dp'=4] {'rows'}, use_global_device_ids=true, to_apply=%region_3.3 | all-reduce | flops 32 | bytes 256 | tf_op jit(solution)/shard_map/while/body/eval_jaxpr/psum | solution.py:40
  438.8 29.0 %psum.41 = f32[1,32]{1,0:T(1,128)S(1)} all-reduce(f32[1,32]{1,0:T(1,128)S(1)} %bitcast.109), channel_id=1, replica_groups=mesh['segment'=8,'rows'=16,'dp'=4] {'rows'}, use_global_device_ids=true, to_apply=%region_6.6 | all-reduce | flops 32 | bytes 256 | tf_op jit(solution)/shard_map/while/body/eval_jaxpr/psum | solution.py:43
  470.0 4.5 collective-permute-start.1
  478.3 1.9 collective-permute-start.2
  480.2 2.3 fusion.108
  486.9 29.3 %psum.40 = f32[1,32]{1,0:T(1,128)S(1)} all-reduce(f32[1,32]{1,0:T(1,128)S(1)} %bitcast.110), channel_id=1, replica_groups=mesh['segment'=8,'rows'=16,'dp'=4] {'rows'}, use_global_device_ids=true, to_apply=%region_3.3 | all-reduce | flops 32 | bytes 256 | tf_op jit(solution)/shard_map/while/body/eval_jaxpr/psum | solution.py:40
  517.4 28.2 %psum.41 = f32[1,32]{1,0:T(1,128)S(1)} all-reduce(f32[1,32]{1,0:T(1,128)S(1)} %bitcast.109), channel_id=1, replica_groups=mesh['segment'=8,'rows'=16,'dp'=4] {'rows'}, use_global_device_ids=true, to_apply=%region_6.6 | all-reduce | flops 32 | bytes 256 | tf_op jit(solution)/shard_map/while/body/eval_jaxpr/psum | solution.py:43
  547.9 4.5 collective-permute-start.1
  558.0 2.3 fusion.108
  564.7 29.3 %psum.40 = f32[1,32]{1,0:T(1,128)S(1)} all-reduce(f32[1,32]{1,0:T(1,128)S(1)} %bitcast.110), channel_id=1, replica_groups=mesh['segment'=8,'rows'=16,'dp'=4] {'rows'}, use_global_device_ids=true, to_apply=%region_3.3 | all-reduce | flops 32 | bytes 256 | tf_op jit(solution)/shard_map/while/body/eval_jaxpr/psum | solution.py:40
  595.2 29.0 %psum.41 = f32[1,32]{1,0:T(1,128)S(1)} all-reduce(f32[1,32]{1,0:T(1,128)S(1)} %bitcast.109), channel_id=1, replica_groups=mesh['segment'=8,'rows'=16,'dp'=4] {'rows'}, use_global_device_ids=true, to_apply=%region_6.6 | all-reduce | flops 32 | bytes 256 | tf_op jit(solution)/shard_map/while/body/eval_jaxpr/psum | solution.py:43
  626.5 4.5 collective-permute-start.1
  636.6 2.3 fusion.108
  643.3 29.3 %psum.40 = f32[1,32]{1,0:T(1,128)S(1)} all-reduce(f32[1,32]{1,0:T(1,128)S(1)} %bitcast.110), channel_id=1, replica_groups=mesh['segment'=8,'rows'=16,'dp'=4] {'rows'}, use_global_device_ids=true, to_apply=%region_3.3 | all-reduce | flops 32 | bytes 256 | tf_op jit(solution)/shard_map/while/body/eval_jaxpr/psum | solution.py:40
  673.8 28.2 %psum.41 = f32[1,32]{1,0:T(1,128)S(1)} all-reduce(f32[1,32]{1,0:T(1,128)S(1)} %bitcast.109), channel_id=1, replica_groups=mesh['segment'=8,'rows'=16,'dp'=4] {'rows'}, use_global_device_ids=true, to_apply=%region_6.6 | all-reduce | flops 32 | bytes 256 | tf_op jit(solution)/shard_map/while/body/eval_jaxpr/psum | solution.py:43
  704.3 4.5 collective-permute-start.1
  714.5 2.3 fusion.108
  721.1 29.3 %psum.40 = f32[1,32]{1,0:T(1,128)S(1)} all-reduce(f32[1,32]{1,0:T(1,128)S(1)} %bitcast.110), channel_id=1, replica_groups=mesh['segment'=8,'rows'=16,'dp'=4] {'rows'}, use_global_device_ids=true, to_apply=%region_3.3 | all-reduce | flops 32 | bytes 256 | tf_op jit(solution)/shard_map/while/body/eval_jaxpr/psum | solution.py:40
  751.6 29.0 %psum.41 = f32[1,32]{1,0:T(1,128)S(1)} all-reduce(f32[1,32]{1,0:T(1,128)S(1)} %bitcast.109), channel_id=1, replica_groups=mesh['segment'=8,'rows'=16,'dp'=4] {'rows'}, use_global_device_ids=true, to_apply=%region_6.6 | all-reduce | flops 32 | bytes 256 | tf_op jit(solution)/shard_map/while/body/eval_jaxpr/psum | solution.py:43
  782.9 4.5 collective-permute-start.1
  793.1 2.3 fusion.108
  799.7 29.3 %psum.40 = f32[1,32]{1,0:T(1,128)S(1)} all-reduce(f32[1,32]{1,0:T(1,128)S(1)} %bitcast.110), channel_id=1, replica_groups=mesh['segment'=8,'rows'=16,'dp'=4] {'rows'}, use_global_device_ids=true, to_apply=%region_3.3 | all-reduce | flops 32 | bytes 256 | tf_op jit(solution)/shard_map/while/body/eval_jaxpr/psum | solution.py:40
  830.2 28.2 %psum.41 = f32[1,32]{1,0:T(1,128)S(1)} all-reduce(f32[1,32]{1,0:T(1,128)S(1)} %bitcast.109), channel_id=1, replica_groups=mesh['segment'=8,'rows'=16,'dp'=4] {'rows'}, use_global_device_ids=true, to_apply=%region_6.6 | all-reduce | flops 32 | bytes 256 | tf_op jit(solution)/shard_map/while/body/eval_jaxpr/psum | solution.py:43
  860.7 4.5 collective-permute-start.1
  870.9 2.3 fusion.108
  875.8 275.4 %all-reduce.3.cloned.1.call-done = f32[3456,128]{1,0:T(8,128)} async-done(((f32[3456,128]{1,0:T(8,128)}), f32[3456,128]{1,0:T(8,128)}) %all-reduce.3.cloned.1.call-update) | async-done | bytes 1769488 | tf_op jit(solution)/shard_map/psum | solution.py:125
  1151.2 2.8 multiply_bitcast_fusion
  (690 shorter events, 137.2 us)
Async XLA Ops:
  7.2 1144.0 %all-reduce.3.cloned.1.call-start = ((), (), s32[]{:S(2)}) async-start(), calls=%async_computation | async-start | bytes 3538944 | tf_op jit(solution)/shard_map/psum | solution.py:125
  76.0 6.5 collective-permute-start
  77.3 5.9 collective-permute-start.1
  83.7 1.2 copy-start
  85.6 5.6 collective-permute-start.2
  155.9 6.5 collective-permute-start
  157.2 5.9 collective-permute-start.1
  163.6 1.2 copy-start
  165.4 5.6 collective-permute-start.2
  233.7 6.5 collective-permute-start
  235.0 5.9 collective-permute-start.1
  241.4 1.2 copy-start
  243.2 5.6 collective-permute-start.2
  312.3 6.5 collective-permute-start
  313.6 5.9 collective-permute-start.1
  320.0 1.2 copy-start
  321.8 5.6 collective-permute-start.2
  390.1 6.5 collective-permute-start
  391.4 5.9 collective-permute-start.1
  397.8 1.2 copy-start
  399.7 5.6 collective-permute-start.2
  468.7 6.5 collective-permute-start
  470.0 5.9 collective-permute-start.1
  476.4 1.2 copy-start
  476.4 1.2 copy-start.5
  478.3 5.6 collective-permute-start.2
  546.6 6.5 collective-permute-start
  547.9 5.9 collective-permute-start.1
  554.3 1.2 copy-start
  556.1 5.6 collective-permute-start.2
  625.2 6.5 collective-permute-start
  626.5 5.9 collective-permute-start.1
  632.9 1.2 copy-start
  634.7 5.6 collective-permute-start.2
  703.0 6.5 collective-permute-start
  704.3 5.9 collective-permute-start.1
  710.7 1.2 copy-start
  712.5 5.6 collective-permute-start.2
  781.6 6.5 collective-permute-start
  782.9 5.9 collective-permute-start.1
  789.3 1.2 copy-start
  791.1 5.6 collective-permute-start.2
  859.4 6.5 collective-permute-start
  860.7 5.9 collective-permute-start.1
  867.1 1.2 copy-start
  869.0 5.6 collective-permute-start.2
  874.5 1.2 copy-start.1
  874.5 279.5 %copy-start.2 = (bf16[4,1,4,8,8,128]{5,4,3,2,1,0:T(8,128)(2,1)}, bf16[4,1,4,8,8,128]{5,4,3,2,1,0:T(8,128)(2,1)S(1)}, u32[]{:S(2)}) copy-start(bf16[4,1,4,8,8,128]{5,4,3,2,1,0:T(8,128)(2,1)S(1)} %get-tuple-element.295) | copy-start | bytes 786436
  (32 other events, 27.3 us)
Sparse Core Ops, SparseCore 0:
  875.9 275.2 all-reduce.2
where the time goes:
time: 1160 us
  blocking collectives  644 us (56%)
  waiting for transfers between devices  299 us (26%)
  starting transfers between devices  85.4 us (7%)
  other arithmetic  58.3 us (5%)
  matrix products  32.1 us (3%)
  local copies, waits for them, and re-layouts  17.7 us (2%)
  between operations  14.1 us (1%)
    psum x11, blocking collectives, statistics(): total = lax.psum(jnp.sum(grouped * mask_six, axis=(1, 2, 3, 5)), 'rows')  331 us
    psum x11, blocking collectives, statistics(): lax.psum(jnp.sum(centered * centered * mask_six, axis=(1, 2, 3, 5)), 'rows')  313 us
    psum x1, waiting for transfers between devices, per_device(): grads = lax.psum(grads, ('rows', 'dp')) * factor  275 us
    ppermute x11, starting transfers between devices, extended_2(): lax.ppermute(tail, axis, [(i, (i + 1) % count) for i in range(ends)])  50 us
    dot_general x11, matrix products, tick(): lax.dot_general(patches, masked, (((0,), (0,)), ((), ())), preferred_elem...  24.9 us
  transfers between devices with their start and end apart: 34, of which 23 were waited for; matrix products, arithmetic and copies ran while one was open for 3% of the time, Pallas kernels for 0%

commit v1 on v0

--- a/solution.py
+++ b/solution.py
@@ -122,7 +122,7 @@
         jnp.zeros((27 * chans, chans), jnp.float32),
     )
     arrived, stash, grads = lax.fori_loop(0, micro + segments - 1, tick, start)
-    grads = lax.psum(grads, ("rows", "dp")) * factor
+    grads = lax.psum(lax.psum(grads, "rows"), "dp") * factor
     return (stash[None], grads[None])
 
 

time: 1160 us -> 1100 us (0.948)
  the two profiles are of different devices: /device:TPU:8 before, /device:TPU:1 now
where the time goes in v1:
time: 1100 us; the launch traced here: 1090 us
  blocking collectives  490 us (45%)
  starting transfers between devices  262 us (24%)
  waiting for transfers between devices  210 us (19%)
  other arithmetic  58.4 us (5%)
  matrix products  32.1 us (3%)
  local copies, waits for them, and re-layouts  17.7 us (2%)
  between operations  14.1 us (1%)
    psum x11, blocking collectives, statistics(): total = lax.psum(jnp.sum(grouped * mask_six, axis=(1, 2, 3, 5)), 'rows')  254 us
    psum x11, blocking collectives, statistics(): lax.psum(jnp.sum(centered * centered * mask_six, axis=(1, 2, 3, 5)), 'rows')  237 us
    psum x2, waiting for transfers between devices, per_device(): grads = lax.psum(lax.psum(grads, 'rows'), 'dp') * factor  208 us
    ppermute x11, starting transfers between devices, passed_along(): return lax.ppermute(block, axis, route)  204 us
    ppermute x11, starting transfers between devices, extended_2(): lax.ppermute(tail, axis, [(i, (i + 1) % count) for i in range(ends)])  43.8 us
    dot_general x11, matrix products, tick(): lax.dot_general(patches, masked, (((0,), (0,)), ((), ())), preferred_elem...  24.9 us
  transfers between devices with their start and end apart: 35, of which 13 were waited for; matrix products, arithmetic and copies ran while one was open for 3% of the time, Pallas kernels for 0%

profile of v1, /device:TPU:1, one launch (start us, length us, event | category | flops | bytes accessed | tf_op | source)
XLA Modules:
  0.0 1094.8 jit_solution(16454320395352553816)
XLA Ops:
  7.3 868.5 %while.20 = (s32[]{:T(128)}, bf16[1,4,8,8,128]{4,3,2,1,0:T(8,128)(2,1)S(1)}, bf16[4,1,4,8,8,128]{5,4,3,2,1,0:T(8,128)(2,1)S(1)}, f32[3456,128]{1,0:T(8,128)S(1)}...) while((s32[]{:T(128)}, ...), condition=%wide.region_7.8_spmd.clone, body=%wide.region_0.7_spmd.clone.sunk | while | flops 457701504 | bytes 18060908 | solution.py:124
  10.4 30.3 %psum.48 = f32[1,32]{1,0:T(1,128)S(1)} all-reduce(f32[1,32]{1,0:T(1,128)S(1)} %bitcast.110), channel_id=1, replica_groups=mesh['segment'=8,'rows'=16,'dp'=4] {'rows'}, use_global_device_ids=true, to_apply=%region_3.3 | all-reduce | flops 32 | bytes 256 | tf_op jit(solution)/shard_map/while/body/eval_jaxpr/psum | solution.py:40
  41.9 20.1 %psum.49 = f32[1,32]{1,0:T(1,128)S(1)} all-reduce(f32[1,32]{1,0:T(1,128)S(1)} %bitcast.109), channel_id=1, replica_groups=mesh['segment'=8,'rows'=16,'dp'=4] {'rows'}, use_global_device_ids=true, to_apply=%region_6.6 | all-reduce | flops 32 | bytes 256 | tf_op jit(solution)/shard_map/while/body/eval_jaxpr/psum | solution.py:43
  64.2 4.0 collective-permute-start.1
  71.3 18.8 %collective-permute-start.2 = (bf16[1,4,8,8,128]{4,3,2,1,0:T(8,128)(2,1)S(1)}, bf16[1,4,8,8,128]{4,3,2,1,0:T(8,128)(2,1)S(1)}, u32[]{:S(2)}, u32[]{:S(2)}) collective-permute-start(bf16[1,4,8,8,128]{4,3,2,1,0:T(8,128)(2,1)S(1)} %get-tuple-element.466), channel_id=1, source_target_pairs={{0,64},{64,128},{128,192},{192,256},{256,320},{320,384},{384,448},... | collective-permute-start | bytes 196616 | tf_op jit(solution)/shard_map/while/body/eval_jaxpr/ppermute | solution.py:31
  95.5 23.3 %psum.48 = f32[1,32]{1,0:T(1,128)S(1)} all-reduce(f32[1,32]{1,0:T(1,128)S(1)} %bitcast.110), channel_id=1, replica_groups=mesh['segment'=8,'rows'=16,'dp'=4] {'rows'}, use_global_device_ids=true, to_apply=%region_3.3 | all-reduce | flops 32 | bytes 256 | tf_op jit(solution)/shard_map/while/body/eval_jaxpr/psum | solution.py:40
  119.9 22.4 %psum.49 = f32[1,32]{1,0:T(1,128)S(1)} all-reduce(f32[1,32]{1,0:T(1,128)S(1)} %bitcast.109), channel_id=1, replica_groups=mesh['segment'=8,'rows'=16,'dp'=4] {'rows'}, use_global_device_ids=true, to_apply=%region_6.6 | all-reduce | flops 32 | bytes 256 | tf_op jit(solution)/shard_map/while/body/eval_jaxpr/psum | solution.py:43
  144.6 4.0 collective-permute-start.1
  151.7 18.3 %collective-permute-start.2 = (bf16[1,4,8,8,128]{4,3,2,1,0:T(8,128)(2,1)S(1)}, bf16[1,4,8,8,128]{4,3,2,1,0:T(8,128)(2,1)S(1)}, u32[]{:S(2)}, u32[]{:S(2)}) collective-permute-start(bf16[1,4,8,8,128]{4,3,2,1,0:T(8,128)(2,1)S(1)} %get-tuple-element.466), channel_id=1, source_target_pairs={{0,64},{64,128},{128,192},{192,256},{256,320},{320,384},{384,448},... | collective-permute-start | bytes 196616 | tf_op jit(solution)/shard_map/while/body/eval_jaxpr/ppermute | solution.py:31
  175.3 22.1 %psum.48 = f32[1,32]{1,0:T(1,128)S(1)} all-reduce(f32[1,32]{1,0:T(1,128)S(1)} %bitcast.110), channel_id=1, replica_groups=mesh['segment'=8,'rows'=16,'dp'=4] {'rows'}, use_global_device_ids=true, to_apply=%region_3.3 | all-reduce | flops 32 | bytes 256 | tf_op jit(solution)/shard_map/while/body/eval_jaxpr/psum | solution.py:40
  198.6 21.5 %psum.49 = f32[1,32]{1,0:T(1,128)S(1)} all-reduce(f32[1,32]{1,0:T(1,128)S(1)} %bitcast.109), channel_id=1, replica_groups=mesh['segment'=8,'rows'=16,'dp'=4] {'rows'}, use_global_device_ids=true, to_apply=%region_6.6 | all-reduce | flops 32 | bytes 256 | tf_op jit(solution)/shard_map/while/body/eval_jaxpr/psum | solution.py:43
  222.3 4.0 collective-permute-start.1
  229.4 18.4 %collective-permute-start.2 = (bf16[1,4,8,8,128]{4,3,2,1,0:T(8,128)(2,1)S(1)}, bf16[1,4,8,8,128]{4,3,2,1,0:T(8,128)(2,1)S(1)}, u32[]{:S(2)}, u32[]{:S(2)}) collective-permute-start(bf16[1,4,8,8,128]{4,3,2,1,0:T(8,128)(2,1)S(1)} %get-tuple-element.466), channel_id=1, source_target_pairs={{0,64},{64,128},{128,192},{192,256},{256,320},{320,384},{384,448},... | collective-permute-start | bytes 196616 | tf_op jit(solution)/shard_map/while/body/eval_jaxpr/ppermute | solution.py:31
  253.2 22.4 %psum.48 = f32[1,32]{1,0:T(1,128)S(1)} all-reduce(f32[1,32]{1,0:T(1,128)S(1)} %bitcast.110), channel_id=1, replica_groups=mesh['segment'=8,'rows'=16,'dp'=4] {'rows'}, use_global_device_ids=true, to_apply=%region_3.3 | all-reduce | flops 32 | bytes 256 | tf_op jit(solution)/shard_map/while/body/eval_jaxpr/psum | solution.py:40
  276.7 22.0 %psum.49 = f32[1,32]{1,0:T(1,128)S(1)} all-reduce(f32[1,32]{1,0:T(1,128)S(1)} %bitcast.109), channel_id=1, replica_groups=mesh['segment'=8,'rows'=16,'dp'=4] {'rows'}, use_global_device_ids=true, to_apply=%region_6.6 | all-reduce | flops 32 | bytes 256 | tf_op jit(solution)/shard_map/while/body/eval_jaxpr/psum | solution.py:43
  300.9 4.0 collective-permute-start.1
  308.0 18.4 %collective-permute-start.2 = (bf16[1,4,8,8,128]{4,3,2,1,0:T(8,128)(2,1)S(1)}, bf16[1,4,8,8,128]{4,3,2,1,0:T(8,128)(2,1)S(1)}, u32[]{:S(2)}, u32[]{:S(2)}) collective-permute-start(bf16[1,4,8,8,128]{4,3,2,1,0:T(8,128)(2,1)S(1)} %get-tuple-element.466), channel_id=1, source_target_pairs={{0,64},{64,128},{128,192},{192,256},{256,320},{320,384},{384,448},... | collective-permute-start | bytes 196616 | tf_op jit(solution)/shard_map/while/body/eval_jaxpr/ppermute | solution.py:31
  331.8 22.3 %psum.48 = f32[1,32]{1,0:T(1,128)S(1)} all-reduce(f32[1,32]{1,0:T(1,128)S(1)} %bitcast.110), channel_id=1, replica_groups=mesh['segment'=8,'rows'=16,'dp'=4] {'rows'}, use_global_device_ids=true, to_apply=%region_3.3 | all-reduce | flops 32 | bytes 256 | tf_op jit(solution)/shard_map/while/body/eval_jaxpr/psum | solution.py:40
  355.3 21.6 %psum.49 = f32[1,32]{1,0:T(1,128)S(1)} all-reduce(f32[1,32]{1,0:T(1,128)S(1)} %bitcast.109), channel_id=1, replica_groups=mesh['segment'=8,'rows'=16,'dp'=4] {'rows'}, use_global_device_ids=true, to_apply=%region_6.6 | all-reduce | flops 32 | bytes 256 | tf_op jit(solution)/shard_map/while/body/eval_jaxpr/psum | solution.py:43
  379.2 4.0 collective-permute-start.1
  386.3 18.0 %collective-permute-start.2 = (bf16[1,4,8,8,128]{4,3,2,1,0:T(8,128)(2,1)S(1)}, bf16[1,4,8,8,128]{4,3,2,1,0:T(8,128)(2,1)S(1)}, u32[]{:S(2)}, u32[]{:S(2)}) collective-permute-start(bf16[1,4,8,8,128]{4,3,2,1,0:T(8,128)(2,1)S(1)} %get-tuple-element.466), channel_id=1, source_target_pairs={{0,64},{64,128},{128,192},{192,256},{256,320},{320,384},{384,448},... | collective-permute-start | bytes 196616 | tf_op jit(solution)/shard_map/while/body/eval_jaxpr/ppermute | solution.py:31
  409.6 22.2 %psum.48 = f32[1,32]{1,0:T(1,128)S(1)} all-reduce(f32[1,32]{1,0:T(1,128)S(1)} %bitcast.110), channel_id=1, replica_groups=mesh['segment'=8,'rows'=16,'dp'=4] {'rows'}, use_global_device_ids=true, to_apply=%region_3.3 | all-reduce | flops 32 | bytes 256 | tf_op jit(solution)/shard_map/while/body/eval_jaxpr/psum | solution.py:40
  433.0 21.8 %psum.49 = f32[1,32]{1,0:T(1,128)S(1)} all-reduce(f32[1,32]{1,0:T(1,128)S(1)} %bitcast.109), channel_id=1, replica_groups=mesh['segment'=8,'rows'=16,'dp'=4] {'rows'}, use_global_device_ids=true, to_apply=%region_6.6 | all-reduce | flops 32 | bytes 256 | tf_op jit(solution)/shard_map/while/body/eval_jaxpr/psum | solution.py:43
  457.0 4.0 collective-permute-start.1
  464.1 18.7 %collective-permute-start.2 = (bf16[1,4,8,8,128]{4,3,2,1,0:T(8,128)(2,1)S(1)}, bf16[1,4,8,8,128]{4,3,2,1,0:T(8,128)(2,1)S(1)}, u32[]{:S(2)}, u32[]{:S(2)}) collective-permute-start(bf16[1,4,8,8,128]{4,3,2,1,0:T(8,128)(2,1)S(1)} %get-tuple-element.466), channel_id=1, source_target_pairs={{0,64},{64,128},{128,192},{192,256},{256,320},{320,384},{384,448},... | collective-permute-start | bytes 196616 | tf_op jit(solution)/shard_map/while/body/eval_jaxpr/ppermute | solution.py:31
  488.2 22.2 %psum.48 = f32[1,32]{1,0:T(1,128)S(1)} all-reduce(f32[1,32]{1,0:T(1,128)S(1)} %bitcast.110), channel_id=1, replica_groups=mesh['segment'=8,'rows'=16,'dp'=4] {'rows'}, use_global_device_ids=true, to_apply=%region_3.3 | all-reduce | flops 32 | bytes 256 | tf_op jit(solution)/shard_map/while/body/eval_jaxpr/psum | solution.py:40
  511.5 20.9 %psum.49 = f32[1,32]{1,0:T(1,128)S(1)} all-reduce(f32[1,32]{1,0:T(1,128)S(1)} %bitcast.109), channel_id=1, replica_groups=mesh['segment'=8,'rows'=16,'dp'=4] {'rows'}, use_global_device_ids=true, to_apply=%region_6.6 | all-reduce | flops 32 | bytes 256 | tf_op jit(solution)/shard_map/while/body/eval_jaxpr/psum | solution.py:43
  534.7 4.0 collective-permute-start.1
  541.8 18.9 %collective-permute-start.2 = (bf16[1,4,8,8,128]{4,3,2,1,0:T(8,128)(2,1)S(1)}, bf16[1,4,8,8,128]{4,3,2,1,0:T(8,128)(2,1)S(1)}, u32[]{:S(2)}, u32[]{:S(2)}) collective-permute-start(bf16[1,4,8,8,128]{4,3,2,1,0:T(8,128)(2,1)S(1)} %get-tuple-element.466), channel_id=1, source_target_pairs={{0,64},{64,128},{128,192},{192,256},{256,320},{320,384},{384,448},... | collective-permute-start | bytes 196616 | tf_op jit(solution)/shard_map/while/body/eval_jaxpr/ppermute | solution.py:31
  566.0 22.1 %psum.48 = f32[1,32]{1,0:T(1,128)S(1)} all-reduce(f32[1,32]{1,0:T(1,128)S(1)} %bitcast.110), channel_id=1, replica_groups=mesh['segment'=8,'rows'=16,'dp'=4] {'rows'}, use_global_device_ids=true, to_apply=%region_3.3 | all-reduce | flops 32 | bytes 256 | tf_op jit(solution)/shard_map/while/body/eval_jaxpr/psum | solution.py:40
  589.3 22.3 %psum.49 = f32[1,32]{1,0:T(1,128)S(1)} all-reduce(f32[1,32]{1,0:T(1,128)S(1)} %bitcast.109), channel_id=1, replica_groups=mesh['segment'=8,'rows'=16,'dp'=4] {'rows'}, use_global_device_ids=true, to_apply=%region_6.6 | all-reduce | flops 32 | bytes 256 | tf_op jit(solution)/shard_map/while/body/eval_jaxpr/psum | solution.py:43
  613.8 4.0 collective-permute-start.1
  620.9 18.4 %collective-permute-start.2 = (bf16[1,4,8,8,128]{4,3,2,1,0:T(8,128)(2,1)S(1)}, bf16[1,4,8,8,128]{4,3,2,1,0:T(8,128)(2,1)S(1)}, u32[]{:S(2)}, u32[]{:S(2)}) collective-permute-start(bf16[1,4,8,8,128]{4,3,2,1,0:T(8,128)(2,1)S(1)} %get-tuple-element.466), channel_id=1, source_target_pairs={{0,64},{64,128},{128,192},{192,256},{256,320},{320,384},{384,448},... | collective-permute-start | bytes 196616 | tf_op jit(solution)/shard_map/while/body/eval_jaxpr/ppermute | solution.py:31
  644.6 22.3 %psum.48 = f32[1,32]{1,0:T(1,128)S(1)} all-reduce(f32[1,32]{1,0:T(1,128)S(1)} %bitcast.110), channel_id=1, replica_groups=mesh['segment'=8,'rows'=16,'dp'=4] {'rows'}, use_global_device_ids=true, to_apply=%region_3.3 | all-reduce | flops 32 | bytes 256 | tf_op jit(solution)/shard_map/while/body/eval_jaxpr/psum | solution.py:40
  668.1 21.1 %psum.49 = f32[1,32]{1,0:T(1,128)S(1)} all-reduce(f32[1,32]{1,0:T(1,128)S(1)} %bitcast.109), channel_id=1, replica_groups=mesh['segment'=8,'rows'=16,'dp'=4] {'rows'}, use_global_device_ids=true, to_apply=%region_6.6 | all-reduce | flops 32 | bytes 256 | tf_op jit(solution)/shard_map/while/body/eval_jaxpr/psum | solution.py:43
  691.5 4.0 collective-permute-start.1
  698.6 18.5 %collective-permute-start.2 = (bf16[1,4,8,8,128]{4,3,2,1,0:T(8,128)(2,1)S(1)}, bf16[1,4,8,8,128]{4,3,2,1,0:T(8,128)(2,1)S(1)}, u32[]{:S(2)}, u32[]{:S(2)}) collective-permute-start(bf16[1,4,8,8,128]{4,3,2,1,0:T(8,128)(2,1)S(1)} %get-tuple-element.466), channel_id=1, source_target_pairs={{0,64},{64,128},{128,192},{192,256},{256,320},{320,384},{384,448},... | collective-permute-start | bytes 196616 | tf_op jit(solution)/shard_map/while/body/eval_jaxpr/ppermute | solution.py:31
  722.5 22.4 %psum.48 = f32[1,32]{1,0:T(1,128)S(1)} all-reduce(f32[1,32]{1,0:T(1,128)S(1)} %bitcast.110), channel_id=1, replica_groups=mesh['segment'=8,'rows'=16,'dp'=4] {'rows'}, use_global_device_ids=true, to_apply=%region_3.3 | all-reduce | flops 32 | bytes 256 | tf_op jit(solution)/shard_map/while/body/eval_jaxpr/psum | solution.py:40
  746.0 21.8 %psum.49 = f32[1,32]{1,0:T(1,128)S(1)} all-reduce(f32[1,32]{1,0:T(1,128)S(1)} %bitcast.109), channel_id=1, replica_groups=mesh['segment'=8,'rows'=16,'dp'=4] {'rows'}, use_global_device_ids=true, to_apply=%region_6.6 | all-reduce | flops 32 | bytes 256 | tf_op jit(solution)/shard_map/while/body/eval_jaxpr/psum | solution.py:43
  770.0 4.0 collective-permute-start.1
  777.1 18.6 %collective-permute-start.2 = (bf16[1,4,8,8,128]{4,3,2,1,0:T(8,128)(2,1)S(1)}, bf16[1,4,8,8,128]{4,3,2,1,0:T(8,128)(2,1)S(1)}, u32[]{:S(2)}, u32[]{:S(2)}) collective-permute-start(bf16[1,4,8,8,128]{4,3,2,1,0:T(8,128)(2,1)S(1)} %get-tuple-element.466), channel_id=1, source_target_pairs={{0,64},{64,128},{128,192},{192,256},{256,320},{320,384},{384,448},... | collective-permute-start | bytes 196616 | tf_op jit(solution)/shard_map/while/body/eval_jaxpr/ppermute | solution.py:31
  801.1 22.2 %psum.48 = f32[1,32]{1,0:T(1,128)S(1)} all-reduce(f32[1,32]{1,0:T(1,128)S(1)} %bitcast.110), channel_id=1, replica_groups=mesh['segment'=8,'rows'=16,'dp'=4] {'rows'}, use_global_device_ids=true, to_apply=%region_3.3 | all-reduce | flops 32 | bytes 256 | tf_op jit(solution)/shard_map/while/body/eval_jaxpr/psum | solution.py:40
  824.5 21.2 %psum.49 = f32[1,32]{1,0:T(1,128)S(1)} all-reduce(f32[1,32]{1,0:T(1,128)S(1)} %bitcast.109), channel_id=1, replica_groups=mesh['segment'=8,'rows'=16,'dp'=4] {'rows'}, use_global_device_ids=true, to_apply=%region_6.6 | all-reduce | flops 32 | bytes 256 | tf_op jit(solution)/shard_map/while/body/eval_jaxpr/psum | solution.py:43
  847.9 4.0 collective-permute-start.1
  855.0 18.6 %collective-permute-start.2 = (bf16[1,4,8,8,128]{4,3,2,1,0:T(8,128)(2,1)S(1)}, bf16[1,4,8,8,128]{4,3,2,1,0:T(8,128)(2,1)S(1)}, u32[]{:S(2)}, u32[]{:S(2)}) collective-permute-start(bf16[1,4,8,8,128]{4,3,2,1,0:T(8,128)(2,1)S(1)} %get-tuple-element.466), channel_id=1, source_target_pairs={{0,64},{64,128},{128,192},{192,256},{256,320},{320,384},{384,448},... | collective-permute-start | bytes 196616 | tf_op jit(solution)/shard_map/while/body/eval_jaxpr/ppermute | solution.py:31
  877.1 131.2 %all-reduce.4.cloned.1.call-done = f32[3456,128]{1,0:T(8,128)} async-done(((f32[3456,128]{1,0:T(8,128)}), f32[3456,128]{1,0:T(8,128)}) %all-reduce.4.cloned.1.call-update) | async-done | bytes 1769488 | tf_op jit(solution)/shard_map/psum | solution.py:125
  1008.4 76.8 %all-reduce.6.cloned.1.call-done = f32[3456,128]{1,0:T(8,128)} async-done(((f32[3456,128]{1,0:T(8,128)}), f32[3456,128]{1,0:T(8,128)}) %all-reduce.6.cloned.1.call-update) | async-done | bytes 1769488 | tf_op jit(solution)/shard_map/psum | solution.py:125
  1085.1 2.8 multiply_bitcast_fusion
  (693 shorter events, 121.5 us)
Async XLA Ops:
  7.2 1001.2 %all-reduce.4.cloned.1.call-start = ((), (), s32[]{:S(2)}) async-start(), calls=%async_computation | async-start | bytes 3538944 | tf_op jit(solution)/shard_map/psum | solution.py:125
  62.9 5.9 collective-permute-start
  64.2 4.8 collective-permute-start.1
  69.5 1.2 copy-start
  71.3 21.1 %collective-permute-start.2 = (bf16[1,4,8,8,128]{4,3,2,1,0:T(8,128)(2,1)S(1)}, bf16[1,4,8,8,128]{4,3,2,1,0:T(8,128)(2,1)S(1)}, u32[]{:S(2)}, u32[]{:S(2)}) collective-permute-start(bf16[1,4,8,8,128]{4,3,2,1,0:T(8,128)(2,1)S(1)} %get-tuple-element.466), channel_id=1, source_target_pairs={{0,64},{64,128},{128,192},{192,256},{256,320},{320,384},{384,448},... | collective-permute-start | bytes 196616 | tf_op jit(solution)/shard_map/while/body/eval_jaxpr/ppermute | solution.py:31
  143.3 5.9 collective-permute-start
  144.6 4.8 collective-permute-start.1
  149.8 1.2 copy-start
  151.7 20.6 %collective-permute-start.2 = (bf16[1,4,8,8,128]{4,3,2,1,0:T(8,128)(2,1)S(1)}, bf16[1,4,8,8,128]{4,3,2,1,0:T(8,128)(2,1)S(1)}, u32[]{:S(2)}, u32[]{:S(2)}) collective-permute-start(bf16[1,4,8,8,128]{4,3,2,1,0:T(8,128)(2,1)S(1)} %get-tuple-element.466), channel_id=1, source_target_pairs={{0,64},{64,128},{128,192},{192,256},{256,320},{320,384},{384,448},... | collective-permute-start | bytes 196616 | tf_op jit(solution)/shard_map/while/body/eval_jaxpr/ppermute | solution.py:31
  221.0 5.9 collective-permute-start
  222.3 4.8 collective-permute-start.1
  227.6 1.2 copy-start
  229.4 20.7 %collective-permute-start.2 = (bf16[1,4,8,8,128]{4,3,2,1,0:T(8,128)(2,1)S(1)}, bf16[1,4,8,8,128]{4,3,2,1,0:T(8,128)(2,1)S(1)}, u32[]{:S(2)}, u32[]{:S(2)}) collective-permute-start(bf16[1,4,8,8,128]{4,3,2,1,0:T(8,128)(2,1)S(1)} %get-tuple-element.466), channel_id=1, source_target_pairs={{0,64},{64,128},{128,192},{192,256},{256,320},{320,384},{384,448},... | collective-permute-start | bytes 196616 | tf_op jit(solution)/shard_map/while/body/eval_jaxpr/ppermute | solution.py:31
  299.6 5.9 collective-permute-start
  300.9 4.8 collective-permute-start.1
  306.2 1.2 copy-start
  308.0 20.7 %collective-permute-start.2 = (bf16[1,4,8,8,128]{4,3,2,1,0:T(8,128)(2,1)S(1)}, bf16[1,4,8,8,128]{4,3,2,1,0:T(8,128)(2,1)S(1)}, u32[]{:S(2)}, u32[]{:S(2)}) collective-permute-start(bf16[1,4,8,8,128]{4,3,2,1,0:T(8,128)(2,1)S(1)} %get-tuple-element.466), channel_id=1, source_target_pairs={{0,64},{64,128},{128,192},{192,256},{256,320},{320,384},{384,448},... | collective-permute-start | bytes 196616 | tf_op jit(solution)/shard_map/while/body/eval_jaxpr/ppermute | solution.py:31
  377.9 5.9 collective-permute-start
  379.2 4.8 collective-permute-start.1
  384.4 1.2 copy-start
  386.3 20.3 %collective-permute-start.2 = (bf16[1,4,8,8,128]{4,3,2,1,0:T(8,128)(2,1)S(1)}, bf16[1,4,8,8,128]{4,3,2,1,0:T(8,128)(2,1)S(1)}, u32[]{:S(2)}, u32[]{:S(2)}) collective-permute-start(bf16[1,4,8,8,128]{4,3,2,1,0:T(8,128)(2,1)S(1)} %get-tuple-element.466), channel_id=1, source_target_pairs={{0,64},{64,128},{128,192},{192,256},{256,320},{320,384},{384,448},... | collective-permute-start | bytes 196616 | tf_op jit(solution)/shard_map/while/body/eval_jaxpr/ppermute | solution.py:31
  455.7 5.9 collective-permute-start
  457.0 4.8 collective-permute-start.1
  462.3 1.2 copy-start
  464.1 21.0 %collective-permute-start.2 = (bf16[1,4,8,8,128]{4,3,2,1,0:T(8,128)(2,1)S(1)}, bf16[1,4,8,8,128]{4,3,2,1,0:T(8,128)(2,1)S(1)}, u32[]{:S(2)}, u32[]{:S(2)}) collective-permute-start(bf16[1,4,8,8,128]{4,3,2,1,0:T(8,128)(2,1)S(1)} %get-tuple-element.466), channel_id=1, source_target_pairs={{0,64},{64,128},{128,192},{192,256},{256,320},{320,384},{384,448},... | collective-permute-start | bytes 196616 | tf_op jit(solution)/shard_map/while/body/eval_jaxpr/ppermute | solution.py:31
  533.4 5.9 collective-permute-start
  534.7 4.8 collective-permute-start.1
  540.0 1.2 copy-start
  541.8 21.2 %collective-permute-start.2 = (bf16[1,4,8,8,128]{4,3,2,1,0:T(8,128)(2,1)S(1)}, bf16[1,4,8,8,128]{4,3,2,1,0:T(8,128)(2,1)S(1)}, u32[]{:S(2)}, u32[]{:S(2)}) collective-permute-start(bf16[1,4,8,8,128]{4,3,2,1,0:T(8,128)(2,1)S(1)} %get-tuple-element.466), channel_id=1, source_target_pairs={{0,64},{64,128},{128,192},{192,256},{256,320},{320,384},{384,448},... | collective-permute-start | bytes 196616 | tf_op jit(solution)/shard_map/while/body/eval_jaxpr/ppermute | solution.py:31
  612.5 5.9 collective-permute-start
  613.8 4.8 collective-permute-start.1
  619.1 1.2 copy-start
  620.9 20.7 %collective-permute-start.2 = (bf16[1,4,8,8,128]{4,3,2,1,0:T(8,128)(2,1)S(1)}, bf16[1,4,8,8,128]{4,3,2,1,0:T(8,128)(2,1)S(1)}, u32[]{:S(2)}, u32[]{:S(2)}) collective-permute-start(bf16[1,4,8,8,128]{4,3,2,1,0:T(8,128)(2,1)S(1)} %get-tuple-element.466), channel_id=1, source_target_pairs={{0,64},{64,128},{128,192},{192,256},{256,320},{320,384},{384,448},... | collective-permute-start | bytes 196616 | tf_op jit(solution)/shard_map/while/body/eval_jaxpr/ppermute | solution.py:31
  690.2 5.9 collective-permute-start
  691.5 4.8 collective-permute-start.1
  696.8 1.2 copy-start
  698.6 20.8 %collective-permute-start.2 = (bf16[1,4,8,8,128]{4,3,2,1,0:T(8,128)(2,1)S(1)}, bf16[1,4,8,8,128]{4,3,2,1,0:T(8,128)(2,1)S(1)}, u32[]{:S(2)}, u32[]{:S(2)}) collective-permute-start(bf16[1,4,8,8,128]{4,3,2,1,0:T(8,128)(2,1)S(1)} %get-tuple-element.466), channel_id=1, source_target_pairs={{0,64},{64,128},{128,192},{192,256},{256,320},{320,384},{384,448},... | collective-permute-start | bytes 196616 | tf_op jit(solution)/shard_map/while/body/eval_jaxpr/ppermute | solution.py:31
  768.7 5.9 collective-permute-start
  770.0 4.8 collective-permute-start.1
  775.3 1.2 copy-start
  777.1 20.9 %collective-permute-start.2 = (bf16[1,4,8,8,128]{4,3,2,1,0:T(8,128)(2,1)S(1)}, bf16[1,4,8,8,128]{4,3,2,1,0:T(8,128)(2,1)S(1)}, u32[]{:S(2)}, u32[]{:S(2)}) collective-permute-start(bf16[1,4,8,8,128]{4,3,2,1,0:T(8,128)(2,1)S(1)} %get-tuple-element.466), channel_id=1, source_target_pairs={{0,64},{64,128},{128,192},{192,256},{256,320},{320,384},{384,448},... | collective-permute-start | bytes 196616 | tf_op jit(solution)/shard_map/while/body/eval_jaxpr/ppermute | solution.py:31
  846.6 5.9 collective-permute-start
  847.9 4.8 collective-permute-start.1
  853.2 1.2 copy-start
  855.0 20.8 %collective-permute-start.2 = (bf16[1,4,8,8,128]{4,3,2,1,0:T(8,128)(2,1)S(1)}, bf16[1,4,8,8,128]{4,3,2,1,0:T(8,128)(2,1)S(1)}, u32[]{:S(2)}, u32[]{:S(2)}) collective-permute-start(bf16[1,4,8,8,128]{4,3,2,1,0:T(8,128)(2,1)S(1)} %get-tuple-element.466), channel_id=1, source_target_pairs={{0,64},{64,128},{128,192},{192,256},{256,320},{320,384},{384,448},... | collective-permute-start | bytes 196616 | tf_op jit(solution)/shard_map/while/body/eval_jaxpr/ppermute | solution.py:31
  875.8 1.2 copy-start.1
  875.9 132.5 %copy-start.2 = (bf16[4,1,4,8,8,128]{5,4,3,2,1,0:T(8,128)(2,1)}, bf16[4,1,4,8,8,128]{5,4,3,2,1,0:T(8,128)(2,1)S(1)}, u32[]{:S(2)}) copy-start(bf16[4,1,4,8,8,128]{5,4,3,2,1,0:T(8,128)(2,1)S(1)} %get-tuple-element.295) | copy-start | bytes 786436
  877.1 208.0 %all-reduce.6.cloned.1.call-start = ((), (), s32[]{:S(2)}) async-start(), calls=%async_computation.1 | async-start | bytes 3538944 | tf_op jit(solution)/shard_map/psum | solution.py:125
  (33 other events, 28.4 us)
Sparse Core Ops, SparseCore 0:
  877.2 131.0 all-reduce.3
  1010.8 74.2 all-reduce.5
